TPU v7x, 256 devices: a whole 4x4x8 slice. The times are simulated.
256 devices in a mesh: aux: 32 (over x, y, core), orb: 8 (over z).
Axes of the slice: x: 4, y: 4, z: 8, core: 2. Of those that a mesh axis runs over, the one named last changes fastest.
Arguments:
- three_index: bfloat16 [64, 192, 128, 128], P('aux', 'orb'), may hold values from -0.5 to 0.5
- home_panels: bfloat16 [32, 20480, 128], P('aux', 'orb')
- panel_owner: int32 [32], replicated, may hold values from 0 to 31, each once
- block_row: int32 [32, 8, 24], P('aux', 'orb'), may hold values from 0 to 19
- block_column: int32 [32, 8, 24], P('aux', 'orb'), may hold values from 0 to 159
- block_count: int32 [32, 8], P('aux', 'orb'), may hold values from 1 to 24, as said below
Outputs:
- exchange_occ: float32 [20480, 256], P('orb', 'aux')
Inputs may be any that keep to these rules, and one draw needn't show every extreme that they name: `block_count`: some aux shard and row shard has all 24 slots live.
All inputs are finite; a program needn't handle non-finite values.
Results may differ from a plain program's by a relative error of at most 0.0037.
Values may be sent and summed in bfloat16 or wider, within the bound.
A program may use at most 64 MiB of HBM per device.

v0:
```python
import jax
import jax.numpy as jnp
from jax import lax
from jax.sharding import PartitionSpec as P

PANELS = 2


def broadcast(value, axis, source):
    kept = jnp.where(lax.axis_index(axis) == source, value, 0).astype(value.dtype)
    return lax.psum(kept, axis)


def body(three_index, home_panels, panel_owner, block_row, block_column, block_count):
    aux_local = three_index.shape[0]
    slot_total = three_index.shape[1]
    block_size = three_index.shape[2]
    rows_local = home_panels.shape[1]
    panel_width = home_panels.shape[2]
    row_blocks = rows_local // block_size
    row_list = block_row[0, 0]
    column_list = block_column[0, 0]
    live_count = block_count[0, 0]
    live_mask = (jnp.arange(slot_total, dtype=jnp.int32) < live_count).astype(jnp.float32)
    placing = (row_list[:, None] == jnp.arange(row_blocks, dtype=jnp.int32)[None, :]).astype(
        jnp.float32
    ) * live_mask[:, None]
    own_home = home_panels[0]
    whole_home = lax.all_gather(own_home, "orb", axis=0, tiled=True)
    panel_parts = []
    local_rows = []
    for panel_index in range(PANELS):
        owner_id = panel_owner[panel_index]
        whole_panel = broadcast(whole_home, "aux", owner_id)
        own_rows = lax.dynamic_slice_in_dim(
            whole_panel, lax.axis_index("orb") * rows_local, rows_local, 0
        )
        tile_grid = whole_panel.reshape(-1, block_size, panel_width)
        picked = tile_grid[column_list]
        products = jnp.einsum(
            "psmk,skj->psmj", three_index, picked, preferred_element_type=jnp.float32
        )
        placed = jnp.einsum("st,psmj->ptmj", placing, products, precision=lax.Precision.HIGHEST)
        panel_parts.append(placed.reshape(aux_local, rows_local, panel_width).astype(jnp.bfloat16))
        local_rows.append(own_rows)
    halfway = jnp.concatenate(panel_parts, axis=2)
    coeff_rows = jnp.concatenate(local_rows, axis=1)
    intersection_part = jnp.einsum(
        "pni,nj->pij", halfway, coeff_rows, preferred_element_type=jnp.float32
    )
    intersection = lax.psum(intersection_part, "orb").astype(jnp.bfloat16)
    exchange_part = jnp.einsum(
        "pmi,pij->mj", halfway, intersection, preferred_element_type=jnp.float32
    )
    return lax.psum_scatter(exchange_part, "aux", scatter_dimension=1, tiled=True)


def solution(mesh):
    placed = (
        P("aux", "orb", None, None),
        P("aux", "orb", None),
        P(),
        P("aux", "orb", None),
        P("aux", "orb", None),
        P("aux", "orb"),
    )
    return jax.shard_map(
        body, mesh=mesh, in_specs=placed, out_specs=P("orb", "aux"), check_vma=False
    )
```

profile of v0, /device:TPU:1, one launch (start us, length us, event | category | flops | bytes accessed | tf_op | source)
XLA Modules:
  0.0 383.5 jit_solution(2066753613081460422)
XLA Ops:
  6.5 0.7 all-gather.3.cloned.1.call-update
  7.3 1.4 fusion.41
  10.0 67.7 %all-gather.3.cloned.1.call-done = bf16[1,20480,128]{2,1,0:T(8,128)(2,1)} async-done(((bf16[1,2560,128]{2,1,0:T(8,128)(2,1)}), bf16[1,20480,128]{2,1,0:T(8,128)(2,1)}) %all-gather.3.cloned.1.call-update) | async-done | bytes 5242896 | tf_op jit(solution)/shard_map/all_gather | solution.py:29
  77.6 6.5 %select_bitcast_fusion.1 = (bf16[20480,128]{1,0:T(8,128)(2,1)}, bf16[20480,128]{1,0:T(8,128)(2,1)}) fusion(bf16[1,20480,128]{2,1,0:T(8,128)(2,1)} %all-gather.3.cloned.1.call-done, pred[]{:T(512)S(6)} %eq.21, pred[]{:T(512)S(6)} %eq.26), kind=kLoop, calls=%fused_computation.3 | loop fusion | flops 5242880 | bytes 15728642 | tf_op jit(solution)/shard_map/jit(_where)/select_n | solution.py:10
  84.2 0.0 reduce-scatter.2.cloned.1.call-start
  85.0 134.0 %all-reduce.4.cloned.1.call-done = (bf16[20480,128]{1,0:T(8,128)(2,1)}, bf16[20480,128]{1,0:T(8,128)(2,1)}) async-done(((bf16[20480,128]{1,0:T(8,128)(2,1)}, bf16[20480,128]{1,0:T(8,128)(2,1)}), (bf16[20480,128]{1,0:T(8,128)(2,1)}, bf16[20480,128]{1,0:T(8,128)(2,1)})) %all-reduce.4.cloned.1.call-update) | async-done | bytes 10485776 | tf_op jit(solution)/shard_map/psum | solution.py:11
  219.0 3.2 gather_fusion
  222.2 2.4 fusion.19
  224.5 3.5 copy.11
  228.1 4.7 %fusion.14 = bf16[2,20,128,128]{3,1,2,0:T(8,128)(2,1)S(1)} fusion(f32[24,128,2,128]{1,0,3,2:T(8,128)} %copy.11, f32[24]{0:T(128)S(1)} %compare_convert_fusion, s32[24]{0:T(128)S(1)} %bitcast.64), kind=kOutput, calls=%fused_computation.14 | convolution fusion | flops 189400000 | bytes 4456640 | tf_op jit(solution)/shard_map/st,psmj->ptmj/dot_general | solution.py:43
  232.8 1.4 copy.7
  234.1 2.2 constant_dynamic-slice_fusion
  236.4 3.2 gather_fusion.1
  239.5 2.2 fusion.17
  241.8 3.6 copy.14
  245.3 4.7 %fusion.11 = bf16[2,20,128,128]{3,1,2,0:T(8,128)(2,1)S(1)} fusion(f32[24,128,2,128]{1,0,3,2:T(8,128)} %copy.14, f32[24]{0:T(128)S(1)} %compare_convert_fusion, s32[24]{0:T(128)S(1)} %bitcast.65), kind=kOutput, calls=%fused_computation.13 | convolution fusion | flops 189400000 | bytes 4456640 | tf_op jit(solution)/shard_map/st,psmj->ptmj/dot_general | solution.py:43
  250.0 0.3 copy.8
  250.4 1.0 copy-done.2
  251.4 0.1 copy-done.1
  251.5 0.5 copy-done.3
  252.0 1.7 fusion.10
  253.7 29.9 %all-reduce.5 = bf16[2,256,256]{1,2,0:T(8,128)(2,1)S(1)} all-reduce(f32[2,256,256]{1,2,0:T(8,128)} %fusion.10), channel_id=1, replica_groups=mesh['aux'=32,'orb'=8] {'orb'}, use_global_device_ids=true, to_apply=%region_2.3 | all-reduce | flops 131072 | bytes 786432 | tf_op jit(solution)/shard_map/psum | solution.py:51
  283.6 3.7 convolution_bitcast_fusion
  287.3 89.6 %reduce-scatter.2.cloned.1.call-done = f32[2560,8]{0,1:T(8,128)} async-done(((f32[2560,256]{0,1:T(8,128)}), f32[2560,8]{0,1:T(8,128)}) %reduce-scatter.2.cloned.1.call-update) | async-done | bytes 81936 | tf_op jit(solution)/shard_map/reduce_scatter | solution.py:55
  (16 shorter events, 0.1 us)
Async XLA Ops:
  6.5 215.6 %copy-start = (bf16[2,24,128,128]{3,2,1,0:T(8,128)(2,1)S(1)}, bf16[2,24,128,128]{3,2,1,0:T(8,128)(2,1)}, u32[]{:S(2)}) copy-start(bf16[2,24,128,128]{3,2,1,0:T(8,128)(2,1)} %param.6) | copy-start | bytes 4718596
  6.5 71.1 %all-gather.3.cloned.1.call-start = ((), (), s32[]{:S(2)}) async-start(), calls=%async_computation.2 | async-start | bytes 5898240 | tf_op jit(solution)/shard_map/all_gather | solution.py:29
  7.3 211.7 %all-reduce.4.cloned.1.call-start = ((), (), s32[]{:S(2)}) async-start(), calls=%async_computation.3 | async-start | bytes 20971520 | tf_op jit(solution)/shard_map/psum | solution.py:11
  84.2 0.7 copy-start.5
  84.2 292.7 %reduce-scatter.2.cloned.1.call-start = ((), (), s32[]{:S(2)}) async-start(), calls=%async_computation.1 | async-start | bytes 2703360 | tf_op jit(solution)/shard_map/reduce_scatter | solution.py:55
  224.5 3.5 copy-start.4
  250.0 1.4 copy-start.1
  250.0 1.9 copy-start.3
  250.4 1.1 copy-start.2
Sparse Core Ops, SparseCore 0:
  9.1 68.4 all-gather.2
  84.3 134.5 all-reduce.3
  287.4 89.4 reduce-scatter.1
where the time goes:
time: 384 us; the launch traced here: 383 us
  waiting for transfers between devices  292 us (76%)
  blocking collectives  29.9 us (8%)
  local copies, waits for them, and re-layouts  20.4 us (5%)
  matrix products  19.4 us (5%)
  between operations  15.2 us (4%)
  other arithmetic  6.56 us (2%)
    psum x1, waiting for transfers between devices, broadcast(): return lax.psum(kept, axis)  134 us
    reduce_scatter x1, waiting for transfers between devices, body(): lax.psum_scatter(exchange_part, 'aux', scatter_dimension=1, tiled=True)  89.6 us
    all_gather x1, waiting for transfers between devices, body(): whole_home = lax.all_gather(own_home, 'orb', axis=0, tiled=True)  67.7 us
    psum x1, blocking collectives, body(): intersection = lax.psum(intersection_part, 'orb').astype(jnp.bfloat16)  29.9 us
    dot_general x2, matrix products, body(): jnp.einsum('st,psmj->ptmj', placing, products, precision=lax.Precision.HI...  9.33 us
  transfers between devices with their start and end apart: 3, of which 3 were waited for; matrix products, arithmetic and copies ran while one was open for 0% of the time, Pallas kernels for 0%

commit v1 on v0

v1 whole, which is shorter than its diff:
```python
import functools

import jax
import jax.numpy as jnp
from jax import lax
from jax.experimental import pallas as pl
from jax.experimental.pallas import tpu as pltpu
from jax.sharding import PartitionSpec as P

MESH = pl.DeviceIdType.MESH
BF16 = jnp.bfloat16
F32 = jnp.float32
BLK = 128
NX, NY, NZ = 4, 4, 8
CHIPS = NX * NY
PLANE = [(dx, dy) for dx in range(NX) for dy in range(NY) if (dx, dy) != (0, 0)]


def here():
    a = lax.axis_index("aux")
    return a // 8, (a // 2) % 4, a % 2, lax.axis_index("orb")


def device(x, y, core, z):
    return ((x * 4 + y) * 2 + core, z)


class Copies:
    def __init__(self, send, recv):
        self.send, self.recv, self.made = send, recv, []

    def start(self, src, dst, target):
        i = len(self.made)
        copy = pltpu.make_async_remote_copy(
            src_ref=src, dst_ref=dst, send_sem=self.send.at[i], recv_sem=self.recv.at[i],
            device_id=target, device_id_type=MESH,
        )
        copy.start()
        self.made.append(copy)
        return copy

    def drain(self):
        for copy in self.made:
            copy.wait_send()


def greet(targets):
    barrier = pltpu.get_barrier_semaphore()
    for target in targets:
        pl.semaphore_signal(barrier, inc=1, device_id=target, device_id_type=MESH)
    return barrier


def peers(x, y, c, z):
    return (
        [device((x + dx) % NX, (y + dy) % NY, c, z) for dx, dy in PLANE]
        + [device(x, y, c, (z + dz) % NZ) for dz in range(1, NZ)]
        + [device(x, y, 1 - c, z)]
    )


GATHER_COPIES = 90


def gather_kernel(owner, home, tri, row, col, cnt, c_out, cl, tri_o, row_o, col_o, cnt_o,
                  land, sel, cand, mine, send, recv, local):
    x, y, c, z = here()
    chip = x * 4 + y
    other = device(x, y, 1 - c, z)
    targets = peers(x, y, c, z)
    barrier = greet(targets)
    keep = pltpu.make_async_copy(home.at[chip], land.at[chip], local.at[0])
    keep.start()
    pl.semaphore_wait(barrier, len(targets))
    net = Copies(send, recv)

    scatter = []
    for dx, dy in PLANE:
        to = ((x + dx) % NX) * 4 + (y + dy) % NY
        scatter.append(net.start(home.at[to], land.at[chip], device((x + dx) % NX, (y + dy) % NY, c, z)))
    swaps = [net.start(tri, tri_o, other), net.start(row, row_o, other), net.start(col, col_o, other),
             net.start(cnt, cnt_o, other)]
    keep.wait()
    for copy in scatter:
        copy.wait_recv()
    sel[...] = land[owner[1 - c] // 2]
    passed = net.start(sel, cand.at[1], other)
    cand[0] = land[owner[c] // 2]
    passed.wait_recv()
    mine[...] = cand[(owner[c] + c) % 2]

    keep = pltpu.make_async_copy(mine, c_out.at[z, chip], local.at[1])
    keep.start()
    column = [net.start(mine, c_out.at[z, chip], device(x, y, c, (z + dz) % NZ)) for dz in range(1, NZ)]
    keep.wait()
    for copy in column:
        copy.wait_recv()

    def piece(h, u, v, first, n):
        u, v = u % 4, v % 4
        return c_out.at[pl.ds(h * 4 + first, n), u * 4 + v if h == 0 else v * 4 + u]

    def at(h, u, v):
        u, v = u % 4, v % 4
        return device(u, v, c, z) if h == 0 else device(v, u, c, z)

    def push(h, src, u, v):
        return net.start(src, src, at(h, u, v))

    uv = [(x, y), (y, x)]
    chunks = {}

    def spread(h, q, du):
        u, v = uv[h]
        src = piece(h, u + du, v, 0, 4)
        chunks[h, q] = [push(h, src, u, v + 1), push(h, src, u, v + 3)]

    def relay(h, q, du):
        u, v = uv[h]
        up, down = chunks[h, q]
        up.wait_recv()
        a = push(h, piece(h, u + du, v + 3, 0, 2), u, v + 1)
        down.wait_recv()
        b = push(h, piece(h, u + du, v + 1, 2, 2), u, v + 3)
        tail.extend([a, b])

    tail = []
    first = {}
    for h in range(2):
        u, v = uv[h]
        src = piece(h, u, v, 0, 4)
        first[h] = [push(h, src, u + 1, v), push(h, src, u + 3, v)]
    for h in range(2):
        spread(h, 0, 0)
    second = {}
    for h in range(2):
        u, v = uv[h]
        first[h][0].wait_recv()
        a = push(h, piece(h, u + 3, v, 0, 2), u + 1, v)
        first[h][1].wait_recv()
        b = push(h, piece(h, u + 1, v, 2, 2), u + 3, v)
        second[h] = [a, b]
        spread(h, 1, 3)
        spread(h, 2, 1)
    for h in range(2):
        relay(h, 0, 0)
    for h in range(2):
        for copy in second[h]:
            copy.wait_recv()
        spread(h, 3, 2)
    for q, du in ((1, 3), (2, 1), (3, 2)):
        for h in range(2):
            relay(h, q, du)
    for copy in tail:
        copy.wait_recv()

    keep = pltpu.make_async_copy(c_out.at[z], cl.at[0], local.at[2])
    keep.start()
    swaps.append(net.start(c_out.at[z], cl.at[1], other))
    keep.wait()
    for copy in swaps:
        copy.wait_recv()
    net.drain()


def half_kernel(row, col, cnt, row_o, col_o, cnt_o, tri, tri_o, blocks, out, cbuf, tbuf, acc, csem, tsem):
    slots = tri.shape[1]
    lists = ((row, col, cnt, tri), (row_o, col_o, cnt_o, tri_o))

    def copies(u, s):
        _, cl, _, t = lists[u]
        return (
            pltpu.make_async_copy(blocks.at[cl[0, 0, s]], cbuf.at[u * slots + s], csem.at[u * slots + s]),
            pltpu.make_async_copy(t.at[:, s], tbuf.at[u * slots + s], tsem.at[u * slots + s]),
        )

    for u in range(2):
        @pl.loop(0, lists[u][2][0, 0])
        def _(s, u=u):
            for copy in copies(u, s):
                copy.start()

    acc[...] = jnp.zeros_like(acc)
    for u in range(2):
        @pl.loop(0, lists[u][2][0, 0])
        def _(s, u=u):
            for copy in copies(u, s):
                copy.wait()
            t = tbuf[u * slots + s].reshape(2 * BLK, BLK)
            prod = lax.dot_general(cbuf[u * slots + s], t, (((0,), (1,)), ((), ())), preferred_element_type=F32)
            at = pl.ds(pl.multiple_of(lists[u][0][0, 0, s] * BLK, BLK), BLK)
            acc[2 * u * BLK:(2 * u + 1) * BLK, at] += prod[:, :BLK]
            acc[(2 * u + 1) * BLK:(2 * u + 2) * BLK, at] += prod[:, BLK:]
    out[...] = acc[...].astype(BF16)


def exchange_kernel(ht, cl, out, ip, rs_land, ifull, itf, eown, eoth, eland, ssend, sland, send, recv):
    x, y, c, z = here()
    other = device(x, y, 1 - c, z)
    targets = peers(x, y, c, z)
    barrier = greet(targets)
    net = Copies(send, recv)
    rows = ht.shape[1]
    tiles = rows // 256

    for j in range(2):
        part = jnp.dot(ht[...], cl[j], preferred_element_type=F32)
        ip[:, :, j * BLK:(j + 1) * BLK] = part.astype(BF16).reshape(NZ, -1, BLK)
    pl.semaphore_wait(barrier, len(targets))
    shares = []
    for dz in range(1, NZ):
        to = (z + dz) % NZ
        shares.append(net.start(ip.at[to], rs_land.at[dz], device(x, y, c, to)))
    total = ip[z].astype(F32)
    for dz in range(1, NZ):
        shares[dz - 1].wait_recv()
        total += rs_land[dz].astype(F32)
    ifull[z] = total.astype(BF16)
    shares = [net.start(ifull.at[z], ifull.at[z], device(x, y, c, (z + dz) % NZ)) for dz in range(1, NZ)]
    for copy in shares:
        copy.wait_recv()

    width = ifull.shape[2]
    inner = ht.shape[0]
    itf[...] = ifull[...].reshape(inner, width).astype(F32).T.reshape(CHIPS, 2, 8, inner)
    it = jnp.concatenate([itf[:, 1 - c].reshape(-1, inner), itf[:, c].reshape(-1, inner)], axis=0).astype(BF16)
    swaps = []
    for t in range(tiles):
        e = jnp.dot(it, ht[:, t * 256:(t + 1) * 256], preferred_element_type=F32)
        e = e.reshape(2, CHIPS, 8, 256)
        e = jnp.concatenate([e[..., :BLK], e[..., BLK:]], axis=2)
        eoth[:, :, t * BLK:(t + 1) * BLK] = e[0].astype(BF16)
        eown[:, :, t * BLK:(t + 1) * BLK] = e[1]
        if t + 1 in (tiles // 2, tiles):
            part = pl.ds((t + 1 - tiles // 2) * BLK, tiles // 2 * BLK)
            swaps.append(net.start(eoth.at[:, :, part], eland.at[:, :, part], other))
    for copy in swaps:
        copy.wait_recv()
    for d in range(CHIPS):
        summed = eown[d] + eland[(d + 8) % CHIPS].astype(F32)
        eown[d] = summed
        ssend[d] = summed.astype(BF16)
    shares = []
    for i, (dx, dy) in enumerate(PLANE):
        to = ((x + dx) % NX) * 4 + (y + dy) % NY
        shares.append(net.start(ssend.at[(to + 8 * c) % CHIPS], sland.at[i],
                                device((x + dx) % NX, (y + dy) % NY, c, z)))
    eown[0] = eown[(x * 4 + y + 8 * c) % CHIPS]
    for i, copy in enumerate(shares):
        copy.wait_recv()
        eown[0] += sland[i].astype(F32)
    for t in range(tiles):
        out[:, t * 256:t * 256 + BLK] = eown[0, 0:8, t * BLK:(t + 1) * BLK]
        out[:, t * 256 + BLK:(t + 1) * 256] = eown[0, 8:16, t * BLK:(t + 1) * BLK]
    net.drain()


def body(three_index, home_panels, panel_owner, block_row, block_column, block_count):
    aux_local, slots = three_index.shape[:2]
    rows, width = home_panels.shape[1:]
    cut = rows // CHIPS
    anywhere = pl.BlockSpec(memory_space=pl.ANY)
    smem = pl.BlockSpec(memory_space=pltpu.SMEM)
    vmem = pl.BlockSpec(memory_space=pltpu.VMEM)
    shape = jax.ShapeDtypeStruct
    dma = pltpu.SemaphoreType.DMA

    panel, local_rows, tri_o, row_o, col_o, cnt_o = pl.pallas_call(
        gather_kernel,
        name="gather",
        out_shape=[
            shape((NZ, CHIPS, cut, width), BF16),
            shape((2, CHIPS, cut, width), BF16),
            shape(three_index.shape, BF16),
            shape(block_row.shape, jnp.int32),
            shape(block_column.shape, jnp.int32),
            shape(block_count.shape, jnp.int32),
        ],
        in_specs=[smem] + [anywhere] * 5,
        out_specs=[anywhere] * 6,
        scratch_shapes=[
            pltpu.VMEM((CHIPS, cut, width), BF16),
            pltpu.VMEM((cut, width), BF16),
            pltpu.VMEM((2, cut, width), BF16),
            pltpu.VMEM((cut, width), BF16),
            dma((GATHER_COPIES,)),
            dma((GATHER_COPIES,)),
            dma((3,)),
        ],
        compiler_params=pltpu.CompilerParams(collective_id=0, has_side_effects=True, vmem_limit_bytes=48 * 2**20),
    )(panel_owner, home_panels.reshape(CHIPS, cut, width), three_index, block_row, block_column, block_count)

    inner = 2 * aux_local * width
    halfway = pl.pallas_call(
        half_kernel,
        name="halfway",
        out_shape=shape((inner, rows), BF16),
        in_specs=[smem] * 6 + [anywhere] * 3,
        out_specs=vmem,
        scratch_shapes=[
            pltpu.VMEM((2 * slots, BLK, width), BF16),
            pltpu.VMEM((2 * slots, aux_local, BLK, BLK), BF16),
            pltpu.VMEM((inner, rows), F32),
            dma((2 * slots,)),
            dma((2 * slots,)),
        ],
        compiler_params=pltpu.CompilerParams(vmem_limit_bytes=48 * 2**20),
    )(block_row, block_column, block_count, row_o, col_o, cnt_o, three_index, tri_o,
      panel.reshape(-1, BLK, width))

    now = 2 * width
    packed = (CHIPS, 16, rows // 2)
    out = pl.pallas_call(
        exchange_kernel,
        name="exchange",
        out_shape=shape((8, rows), F32),
        in_specs=[vmem, vmem],
        out_specs=vmem,
        scratch_shapes=[
            pltpu.VMEM((NZ, inner // NZ, now), BF16),
            pltpu.VMEM((NZ, inner // NZ, now), BF16),
            pltpu.VMEM((NZ, inner // NZ, now), BF16),
            pltpu.VMEM((CHIPS, 2, 8, inner), F32),
            pltpu.VMEM(packed, F32),
            pltpu.VMEM(packed, BF16),
            pltpu.VMEM(packed, BF16),
            pltpu.VMEM(packed, BF16),
            pltpu.VMEM((CHIPS - 1,) + packed[1:], BF16),
            dma((31,)),
            dma((31,)),
        ],
        compiler_params=pltpu.CompilerParams(collective_id=1, has_side_effects=True, vmem_limit_bytes=48 * 2**20),
    )(halfway, local_rows.reshape(2, rows, width))
    return out.T


def solution(mesh):
    placed = (
        P("aux", "orb", None, None),
        P("aux", "orb", None),
        P(),
        P("aux", "orb", None),
        P("aux", "orb", None),
        P("aux", "orb"),
    )
    return jax.shard_map(
        body, mesh=mesh, in_specs=placed, out_specs=P("orb", "aux"), check_vma=False
    )
```

time: 384 us -> 123 us (0.32)
  waiting for transfers between devices: 292 us -> 0 us
  Pallas kernels: 0 us -> 117 us
  blocking collectives: 29.9 us -> 0 us
  matrix products: 19.4 us -> 0 us
  local copies, waits for them, and re-layouts: 20.4 us -> 5.1 us
  between operations: 15.2 us -> 0.72 us
  other arithmetic: 6.56 us -> 0 us
    psum x1 -> x0, waiting for transfers between devices: 134 us -> none  [broadcast(): return lax.psum(kept, axis)]
    pallas_call x0 -> x3, Pallas kernels: none -> 117 us  [the longest x1 67.8 us: body(): pl.pallas_call(gather_kernel, name='gather', out_shape=[shape((NZ, CHIPS,...]
    reduce_scatter x1 -> x0, waiting for transfers between devices: 89.6 us -> none  [body(): lax.psum_scatter(exchange_part, 'aux', scatter_dimension=1, tiled=True)]
    all_gather x1 -> x0, waiting for transfers between devices: 67.7 us -> none  [body(): whole_home = lax.all_gather(own_home, 'orb', axis=0, tiled=True)]
    psum x1 -> x0, blocking collectives: 29.9 us -> none  [body(): intersection = lax.psum(intersection_part, 'orb').astype(jnp.bfloat16)]
    dot_general x6 -> x0, matrix products: 19.4 us -> none  [the longest x2 9.33 us: body(): jnp.einsum('st,psmj->ptmj', placing, products, precision=lax.Precision.HI...]
    dot_general x2 -> x0, local copies, waits for them, and re-layouts: 7.08 us -> none  [body(): jnp.einsum('psmk,skj->psmj', three_index, picked, preferred_element_type=...]
    select_n x2 -> x0, other arithmetic: 6.55 us -> none  [the longest x1 6.55 us: broadcast(): jnp.where(lax.axis_index(axis) == source, value, 0).astype(value.dtype)]
  transfers between devices with their start and end apart: 3 -> 0, of which waited for: 3 -> 0; matrix products, arithmetic and copies ran while one was open for 0% -> 0% of each run, Pallas kernels for 0% -> 0%
where the time goes in v1:
time: 123 us; the launch traced here: 122 us
  Pallas kernels  117 us (95%)
  local copies, waits for them, and re-layouts  5.1 us (4%)
    pallas_call x1, Pallas kernels, body(): pl.pallas_call(gather_kernel, name='gather', out_shape=[shape((NZ, CHIPS,...  67.8 us
    pallas_call x1, Pallas kernels, body(): pl.pallas_call(exchange_kernel, name='exchange', out_shape=shape((8, rows...  42.1 us
    pallas_call x1, Pallas kernels, body(): pl.pallas_call(half_kernel, name='halfway', out_shape=shape((inner, rows)...  6.65 us
    unnamed x15, local copies, waits for them, and re-layouts  5.1 us

profile of v1, /device:TPU:1, one launch (start us, length us, event | category | flops | bytes accessed | tf_op | source)
XLA Modules:
  0.0 122.3 jit_solution(9205155070716806629)
XLA Ops:
  0.0 0.0 copy-start.5
  0.7 0.0 copy-start
  0.7 1.4 %copy-done = bf16[2,24,128,128]{3,2,1,0:T(8,128)(2,1)S(1)} copy-done((bf16[2,24,128,128]{3,2,1,0:T(8,128)(2,1)S(1)}, bf16[2,24,128,128]{3,2,1,0:T(8,128)(2,1)}, u32[]{:S(2)}) %copy-start) | copy-done | bytes 1572888
  2.1 0.0 copy-start.2
  2.1 1.1 copy-done.2
  3.2 0.0 copy-start.3
  3.2 0.7 copy-done.3
  3.8 0.0 copy-start.4
  3.8 0.7 copy-done.4
  4.5 0.0 copy-start.6
  4.5 0.7 copy-done.6
  5.1 0.0 copy-start.1
  5.1 67.8 %gather.1 = (bf16[8,16,160,128]{3,2,1,0:T(8,128)(2,1)}, bf16[2,16,160,128]{3,2,1,0:T(8,128)(2,1)S(1)}, bf16[2,24,128,128]{3,2,1,0:T(8,128)(2,1)S(1)}, s32[1,1,24...) custom-call(s32[32]{0:T(128)S(1)} %copy-done.6, bf16[16,160,128]{2,1,0:T(8,128)(2,1)S(1)} %bitcast.5, ...), custom_call_target="tpu_custom_call" | custom-call | tf_op jit(solution)/shard_map/gather/pallas_call | solution.py:268
  72.9 0.0 copy-done.5
  72.9 0.0 copy-done.1
  72.9 6.6 %halfway.1.ht = bf16[512,2560]{1,0:T(8,128)(2,1)S(1)} custom-call(s32[1,1,24]{2,1,0:T(1,128)S(1)} %copy-done.3, s32[1,1,24]{2,1,0:T(1,128)S(1)} %copy-done.5, s32[1,1]{1,0:T(1,128)S(6)} %copy.8.cnt, s32[1,1,24]{2,1,0:T(1,128)S(1)} %get-tuple-element.11.row_o, s32[1,1,24]{2,1,0:T(1,128)S(1)} %get-tuple-element.12.col_o, s32[1,1]{1,0:T(1,128)} %get-tuple-element.13.cnt_o, ...), custom_call_target="tpu_custom_call" | custom-call | tf_op jit(solution)/shard_map/halfway/pallas_call | solution.py:294
  79.6 42.1 %exchange.1 = f32[8,2560]{1,0:T(8,128)S(1)} custom-call(bf16[512,2560]{1,0:T(8,128)(2,1)S(1)} %halfway.1.ht, bf16[2,2560,128]{2,1,0:T(8,128)(2,1)S(1)} %bitcast.4), custom_call_target="tpu_custom_call" | custom-call | tf_op jit(solution)/shard_map/exchange/pallas_call | solution.py:313
  121.7 0.6 copy.9
Async XLA Ops:
  0.0 72.9 %copy-start.5 = (s32[1,1,24]{2,1,0:T(1,128)S(1)}, s32[1,1,24]{2,1,0:T(1,128)}, u32[]{:S(2)}) copy-start(s32[1,1,24]{2,1,0:T(1,128)} %col.3) | copy-start | bytes 292
  0.7 1.4 %copy-start = (bf16[2,24,128,128]{3,2,1,0:T(8,128)(2,1)S(1)}, bf16[2,24,128,128]{3,2,1,0:T(8,128)(2,1)}, u32[]{:S(2)}) copy-start(bf16[2,24,128,128]{3,2,1,0:T(8,128)(2,1)} %tri.3) | copy-start | bytes 4718596
  2.1 1.1 copy-start.2
  3.2 0.7 copy-start.3
  3.8 0.7 copy-start.4
  4.5 0.7 copy-start.6
  5.1 67.8 %copy-start.1 = (bf16[2,24,128,128]{3,2,1,0:T(8,128)(2,1)S(1)}, bf16[2,24,128,128]{3,2,1,0:T(8,128)(2,1)}, u32[]{:S(2)}) copy-start(bf16[2,24,128,128]{3,2,1,0:T(8,128)(2,1)} %tri.3) | copy-start | bytes 4718596

commit v2 on v0

v2 whole, which is shorter than its diff:
```python
import functools

import jax
import jax.numpy as jnp
from jax import lax
from jax.experimental import pallas as pl
from jax.experimental.pallas import tpu as pltpu
from jax.sharding import PartitionSpec as P

MESH = pl.DeviceIdType.MESH
BF16 = jnp.bfloat16
F32 = jnp.float32
BLK = 128
NX, NY, NZ = 4, 4, 8
CHIPS = NX * NY
PLANE = [(dx, dy) for dx in range(NX) for dy in range(NY) if (dx, dy) != (0, 0)]
ROWS = 2560
SLOTS = 24
ROW_BLOCKS = ROWS // BLK
RING = 8
LAST = ROW_BLOCKS - RING
INNER = 512
TILE = 256
TILES = ROWS // TILE
PARTS = 2
COPIES = 180


def here():
    a = lax.axis_index("aux")
    return a // 8, (a // 2) % 4, a % 2, lax.axis_index("orb")


def device(x, y, core, z):
    return ((x * 4 + y) * 2 + core, z)


class Copies:
    def __init__(self, send, recv):
        self.send, self.recv, self.made = send, recv, []

    def start(self, src, dst, target):
        i = len(self.made)
        copy = pltpu.make_async_remote_copy(
            src_ref=src, dst_ref=dst, send_sem=self.send.at[i], recv_sem=self.recv.at[i],
            device_id=target, device_id_type=MESH,
        )
        copy.start()
        self.made.append(copy)
        return copy

    def drain(self):
        for copy in self.made:
            copy.wait_send()


def peers(x, y, c, z):
    return (
        [device((x + dx) % NX, (y + dy) % NY, c, z) for dx, dy in PLANE]
        + [device(x, y, c, (z + dz) % NZ) for dz in range(1, NZ)]
        + [device(x, y, 1 - c, z)]
    )


def wait(copies):
    for copy in copies:
        copy.wait_recv()


def kernel(owner, home, tri, row, col, cnt, out,
           panel, land0, land1, sel0, sel1, cand0, cand1, own_t, other_t, lists_v, cnt_v, row_s, col_s, cnt_s, prev, last, run, half,
           other_rows, ip, ip_land, ifull, itf, eown, eoth, eland, ssend, sland, send, recv, local):
    land, sel, cand = (land0, land1), (sel0, sel1), (cand0, cand1)
    x, y, c, z = here()
    chip = x * 4 + y
    other = device(x, y, 1 - c, z)
    targets = peers(x, y, c, z)
    barrier = pltpu.get_barrier_semaphore()
    for target in targets:
        pl.semaphore_signal(barrier, inc=1, device_id=target, device_id_type=MESH)
    net = Copies(send, recv)

    def piece(p, j):
        if p == 0:
            return pl.ds(j // 2, 1), pl.ds(j % 2 * 64, 64)
        return pl.ds(RING + j // 4 * (LAST // 4), LAST // 4), pl.ds(j % 4 * 32, 32)

    here_copies = [
        pltpu.make_async_copy(home.at[piece(0, chip)], land[0].at[chip], local.at[0]),
        pltpu.make_async_copy(home.at[piece(1, chip)], land[1].at[chip], local.at[1]),
        pltpu.make_async_copy(row, row_s.at[0], local.at[2]),
        pltpu.make_async_copy(col, col_s.at[0], local.at[3]),
        pltpu.make_async_copy(cnt, cnt_s.at[0], local.at[4]),
        pltpu.make_async_copy(tri, own_t, local.at[5]),
    ]
    for copy in here_copies:
        copy.start()
    pl.semaphore_wait(barrier, len(targets))

    scatter = []
    for p in range(2):
        scatter.append([])
        for dx, dy in PLANE:
            tx, ty = (x + dx) % NX, (y + dy) % NY
            scatter[p].append(net.start(
                home.at[piece(p, tx * 4 + ty)], land[p].at[chip], device(tx, ty, c, z)))
        if p == 0:
            row_copy = net.start(row, lists_v.at[0], other)
            col_copy = net.start(col, lists_v.at[1], other)
            cnt_copy = net.start(cnt, cnt_v, other)
    tri_copy = net.start(tri, other_t, other)

    wait([row_copy, col_copy, cnt_copy])
    to_smem = [
        pltpu.make_async_copy(lists_v.at[0], row_s.at[1], local.at[6]),
        pltpu.make_async_copy(lists_v.at[1], col_s.at[1], local.at[7]),
        pltpu.make_async_copy(cnt_v, cnt_s.at[1], local.at[8]),
    ]
    for copy in to_smem:
        copy.start()
    for copy in here_copies[2:5] + to_smem:
        copy.wait()
    for u in range(2):
        @pl.loop(0, SLOTS)
        def _(s, u=u):
            mine = row_s[u, 0, 0, s]
            found = jnp.int32(SLOTS)
            for e in range(SLOTS - 1):
                same = jnp.logical_and(row_s[u, 0, 0, e] == mine, e < s)
                found = jnp.where(same, jnp.int32(e), found)
            prev[u, s] = found

        @pl.loop(0, ROW_BLOCKS)
        def _(t, u=u):
            found = jnp.int32(SLOTS)
            for e in range(SLOTS):
                same = jnp.logical_and(row_s[u, 0, 0, e] == t, e < cnt_s[u, 0, 0])
                found = jnp.where(same, jnp.int32(e), found)
            last[u, t] = found

        run[u, SLOTS] = jnp.zeros((2 * BLK, BLK), F32)

    def choose(p):
        here_copies[p].wait()
        wait(scatter[p])
        sel[p][...] = land[p][owner[1 - c] // 2]
        passed = net.start(sel[p], cand[p].at[1], other)
        cand[p][0] = land[p][owner[c] // 2]
        passed.wait_recv()
        panel[(z,) + piece(p, chip)] = cand[p][(owner[c] + c) % 2]

    choose(0)
    mine = panel.at[(z,) + piece(0, chip)]
    plane = [net.start(mine, mine, device((x + dx) % NX, (y + dy) % NY, c, z)) for dx, dy in PLANE]
    choose(1)
    mine = panel.at[(z,) + piece(1, chip)]
    column = [net.start(mine, mine, device(x, y, c, (z + dz) % NZ)) for dz in range(1, NZ)]

    ring = {}

    def step(k, e):
        for sign in (1, -1):
            far = 4 if (sign == 1) == (e == 0) else 3
            if k > far:
                continue
            if k > 1:
                ring[k - 1, e, sign].wait_recv()
            at = (z - sign * (k - 1)) % NZ
            src = panel.at[at, pl.ds(e * (RING // 2), RING // 2)]
            ring[k, e, sign] = net.start(src, src, device(x, y, c, (z + sign) % NZ))

    wait(plane)
    step(1, 0)
    step(1, 1)
    swaps = [net.start(panel.at[z, pl.ds(0, RING)], other_rows.at[pl.ds(0, RING)], other)]

    def block(h, u, v, first, n):
        u, v = u % 4, v % 4
        return panel.at[(pl.ds(h * 4 + first, n),) + piece(1, u * 4 + v if h == 0 else v * 4 + u)]

    def push(h, src, u, v):
        u, v = u % 4, v % 4
        return net.start(src, src, device(u, v, c, z) if h == 0 else device(v, u, c, z))

    uv = [(x, y), (y, x)]
    chunks, first, second, tail = {}, {}, {}, []

    def spread(h, q, du):
        u, v = uv[h]
        src = block(h, u + du, v, 0, 4)
        chunks[h, q] = [push(h, src, u, v + 1), push(h, src, u, v + 3)]

    def relay(h, q, du):
        u, v = uv[h]
        up, down = chunks[h, q]
        up.wait_recv()
        tail.append(push(h, block(h, u + du, v + 3, 0, 2), u, v + 1))
        down.wait_recv()
        tail.append(push(h, block(h, u + du, v + 1, 2, 2), u, v + 3))

    wait(column)
    for h in range(2):
        u, v = uv[h]
        src = block(h, u, v, 0, 4)
        first[h] = [push(h, src, u + 1, v), push(h, src, u + 3, v)]
    for h in range(2):
        spread(h, 0, 0)
    step(2, 0)
    for h in range(2):
        u, v = uv[h]
        first[h][0].wait_recv()
        second[h] = [push(h, block(h, u + 3, v, 0, 2), u + 1, v)]
        first[h][1].wait_recv()
        second[h].append(push(h, block(h, u + 1, v, 2, 2), u + 3, v))
        spread(h, 1, 3)
        spread(h, 2, 1)
    step(2, 1)
    for h in range(2):
        relay(h, 0, 0)
    step(3, 0)
    for h in range(2):
        wait(second[h])
        spread(h, 3, 2)
    for h in range(2):
        relay(h, 1, 3)
    step(3, 1)
    for h in range(2):
        relay(h, 2, 1)
    step(4, 0)
    step(4, 1)
    for h in range(2):
        relay(h, 3, 2)
    wait(tail)
    swaps.append(net.start(panel.at[z, pl.ds(RING, LAST)], other_rows.at[pl.ds(RING, LAST)], other))
    wait([ring[3, 0, -1], ring[3, 1, 1], ring[4, 0, 1], ring[4, 1, -1]])

    here_copies[5].wait()
    tri_copy.wait_recv()
    for u, integrals in enumerate((own_t, other_t)):
        @pl.loop(0, SLOTS, step=2)
        def _(s0, u=u, integrals=integrals):
            products = []
            for i in range(2):
                b = col_s[u, 0, 0, s0 + i]
                rows = panel[b // ROW_BLOCKS, b % ROW_BLOCKS]
                t = integrals[:, s0 + i].reshape(2 * BLK, BLK)
                products.append(jnp.dot(t, rows, preferred_element_type=F32))
            for i in range(2):
                run[u, s0 + i] = products[i] + run[u, prev[u, s0 + i]]
    for u in range(2):
        @pl.loop(0, ROW_BLOCKS)
        def _(t, u=u):
            total = run[u, last[u, t]].astype(BF16)
            at = pl.ds(pl.multiple_of(t * BLK, BLK), BLK)
            for p in range(2):
                half[at, pl.ds((2 * u + p) * BLK, BLK)] = total[p * BLK:(p + 1) * BLK]

    wait(swaps)
    for j in range(2):
        rows = (panel[z] if j == 0 else other_rows[...]).reshape(ROWS, BLK)
        part = lax.dot_general(rows, half[...], (((0,), (0,)), ((), ())), preferred_element_type=F32)
        ip[j * 4:(j + 1) * 4] = part.astype(BF16).reshape(4, 32, INNER)
    shares = []
    for dz in range(1, NZ):
        to = (z + dz) % NZ
        shares.append(net.start(ip.at[to], ip_land.at[dz - 1], device(x, y, c, to)))
    total = ip[z].astype(F32)
    for dz in range(1, NZ):
        shares[dz - 1].wait_recv()
        total += ip_land[dz - 1].astype(F32)
    ifull[z] = total.astype(BF16)
    wait([net.start(ifull.at[z], ifull.at[z], device(x, y, c, (z + dz) % NZ)) for dz in range(1, NZ)])

    itf[...] = ifull[...].astype(F32).reshape(CHIPS, 2, 8, INNER)
    it = jnp.concatenate([itf[:, 1 - c].reshape(-1, INNER), itf[:, c].reshape(-1, INNER)], axis=0).astype(BF16)
    per = TILES // PARTS
    swaps = []
    for t in range(TILES):
        e = lax.dot_general(it, half[t * TILE:(t + 1) * TILE, :], (((1,), (1,)), ((), ())),
                            preferred_element_type=F32)
        e = e.reshape(2, CHIPS, 8, TILE)
        e = jnp.concatenate([e[..., :BLK], e[..., BLK:]], axis=2)
        eoth[t // per, :, :, t % per * BLK:(t % per + 1) * BLK] = e[0].astype(BF16)
        eown[t // per, :, :, t % per * BLK:(t % per + 1) * BLK] = e[1]
        if (t + 1) % per == 0:
            swaps.append(net.start(eoth.at[t // per], eland.at[t // per], other))
    shares = []
    for k in range(PARTS):
        swaps[k].wait_recv()
        for d in range(CHIPS):
            summed = eown[k, d] + eland[k, (d + 8) % CHIPS].astype(F32)
            eown[k, d] = summed
            ssend[k, d] = summed.astype(BF16)
        shares.append([])
        for i, (dx, dy) in enumerate(PLANE):
            tx, ty = (x + dx) % NX, (y + dy) % NY
            shares[k].append(net.start(ssend.at[k, (tx * 4 + ty + 8 * c) % CHIPS], sland.at[k, i],
                                       device(tx, ty, c, z)))
    for k in range(PARTS):
        total = eown[k, (chip + 8 * c) % CHIPS]
        for i, copy in enumerate(shares[k]):
            copy.wait_recv()
            total += sland[k, i].astype(F32)
        for t in range(per):
            at = (k * per + t) * TILE
            out[:, at:at + BLK] = total[0:8, t * BLK:(t + 1) * BLK]
            out[:, at + BLK:at + TILE] = total[8:16, t * BLK:(t + 1) * BLK]
    net.drain()


def body(three_index, home_panels, panel_owner, block_row, block_column, block_count):
    anywhere = pl.BlockSpec(memory_space=pl.ANY)
    smem = pl.BlockSpec(memory_space=pltpu.SMEM)
    dma = pltpu.SemaphoreType.DMA
    vm = pltpu.VMEM
    pieces = (1, 64, BLK), (LAST // 4, 32, BLK)
    packed = (PARTS, CHIPS, 16, ROWS // 2 // PARTS)
    out = pl.pallas_call(
        kernel,
        name="exchange",
        out_shape=jax.ShapeDtypeStruct((8, ROWS), F32),
        in_specs=[smem] + [anywhere] * 5,
        out_specs=pl.BlockSpec(memory_space=vm),
        scratch_shapes=[
            vm((NZ, ROW_BLOCKS, BLK, BLK), BF16),
            vm((CHIPS,) + pieces[0], BF16),
            vm((CHIPS,) + pieces[1], BF16),
            vm(pieces[0], BF16),
            vm(pieces[1], BF16),
            vm((2,) + pieces[0], BF16),
            vm((2,) + pieces[1], BF16),
            vm(three_index.shape, BF16),
            vm(three_index.shape, BF16),
            vm((2,) + block_row.shape, jnp.int32),
            vm(block_count.shape, jnp.int32),
            pltpu.SMEM((2,) + block_row.shape, jnp.int32),
            pltpu.SMEM((2,) + block_row.shape, jnp.int32),
            pltpu.SMEM((2,) + block_count.shape, jnp.int32),
            pltpu.SMEM((2, SLOTS), jnp.int32),
            pltpu.SMEM((2, ROW_BLOCKS), jnp.int32),
            vm((2, SLOTS + 1, 2 * BLK, BLK), F32),
            vm((ROWS, INNER), BF16),
            vm((ROW_BLOCKS, BLK, BLK), BF16),
            vm((NZ, 32, INNER), BF16),
            vm((NZ - 1, 32, INNER), BF16),
            vm((NZ, 32, INNER), BF16),
            vm((CHIPS, 2, 8, INNER), F32),
            vm(packed, F32),
            vm(packed, BF16),
            vm(packed, BF16),
            vm(packed, BF16),
            vm((PARTS, CHIPS - 1) + packed[2:], BF16),
            dma((COPIES,)),
            dma((COPIES,)),
            dma((9,)),
        ],
        compiler_params=pltpu.CompilerParams(collective_id=0, has_side_effects=True, vmem_limit_bytes=60 * 2**20),
    )(panel_owner, home_panels.reshape(ROW_BLOCKS, BLK, BLK), three_index, block_row, block_column, block_count)
    return out.T


def solution(mesh):
    placed = (
        P("aux", "orb", None, None),
        P("aux", "orb", None),
        P(),
        P("aux", "orb", None),
        P("aux", "orb", None),
        P("aux", "orb"),
    )
    return jax.shard_map(
        body, mesh=mesh, in_specs=placed, out_specs=P("orb", "aux"), check_vma=False
    )
```

time: 384 us -> 92.2 us (0.24)
  waiting for transfers between devices: 292 us -> 0 us
  Pallas kernels: 0 us -> 89.8 us
  blocking collectives: 29.9 us -> 0 us
  matrix products: 19.4 us -> 0 us
  local copies, waits for them, and re-layouts: 20.4 us -> 1.53 us
  between operations: 15.2 us -> 0.66 us
  other arithmetic: 6.56 us -> 0 us
    psum x1 -> x0, waiting for transfers between devices: 134 us -> none  [broadcast(): return lax.psum(kept, axis)]
    pallas_call x0 -> x1, Pallas kernels: none -> 89.8 us  [body(): pl.pallas_call(kernel, name='exchange', out_shape=jax.ShapeDtypeStruct((8...]
    reduce_scatter x1 -> x0, waiting for transfers between devices: 89.6 us -> none  [body(): lax.psum_scatter(exchange_part, 'aux', scatter_dimension=1, tiled=True)]
    all_gather x1 -> x0, waiting for transfers between devices: 67.7 us -> none  [body(): whole_home = lax.all_gather(own_home, 'orb', axis=0, tiled=True)]
    psum x1 -> x0, blocking collectives: 29.9 us -> none  [body(): intersection = lax.psum(intersection_part, 'orb').astype(jnp.bfloat16)]
    dot_general x6 -> x0, matrix products: 19.4 us -> none  [the longest x2 9.33 us: body(): jnp.einsum('st,psmj->ptmj', placing, products, precision=lax.Precision.HI...]
    dot_general x2 -> x0, local copies, waits for them, and re-layouts: 7.08 us -> none  [body(): jnp.einsum('psmk,skj->psmj', three_index, picked, preferred_element_type=...]
    select_n x2 -> x0, other arithmetic: 6.55 us -> none  [the longest x1 6.55 us: broadcast(): jnp.where(lax.axis_index(axis) == source, value, 0).astype(value.dtype)]
  transfers between devices with their start and end apart: 3 -> 0, of which waited for: 3 -> 0; matrix products, arithmetic and copies ran while one was open for 0% -> 0% of each run, Pallas kernels for 0% -> 0%
where the time goes in v2:
time: 92.2 us; the launch traced here: 92 us
  Pallas kernels  89.8 us (97%)
  local copies, waits for them, and re-layouts  1.53 us (2%)
    pallas_call x1, Pallas kernels, body(): pl.pallas_call(kernel, name='exchange', out_shape=jax.ShapeDtypeStruct((8...  89.8 us

profile of v2, /device:TPU:1, one launch (start us, length us, event | category | flops | bytes accessed | tf_op | source)
XLA Modules:
  0.0 92.0 jit_solution(11713288720075542351)
XLA Ops:
  0.7 89.8 %exchange.1 = f32[8,2560]{1,0:T(8,128)} custom-call(s32[32]{0:T(128)} %owner.1, bf16[20,128,128]{2,1,0:T(8,128)(2,1)} %bitcast.2, bf16[2,24,128,128]{3,2,1,0:T(8,128)(2,1)} %tri.1, s32[1,1,24]{2,1,0:T(1,128)} %row.1, s32[1,1,24]{2,1,0:T(1,128)} %col.1, s32[1,1]{1,0:T(1,128)S(6)} %copy.8.cnt), custom_call_target="tpu_custom_call" | custom-call | tf_op jit(solution)/shard_map/exchange/pallas_call | solution.py:318
  90.5 1.5 %copy.9 = f32[2560,8]{0,1:T(8,128)} copy(f32[2560,8]{0,1:T(8,128)} %bitcast.3) | data formatting | bytes 163840

commit v3 on v2

v3 whole, which is shorter than its diff:
```python
import math

import jax
import jax.numpy as jnp
from jax import lax
from jax.experimental import pallas as pl
from jax.experimental.pallas import tpu as pltpu
from jax.sharding import PartitionSpec as P

MESH = pl.DeviceIdType.MESH
BF16 = jnp.bfloat16
F32 = jnp.float32
BLK = 128
NX, NY, NZ = 4, 4, 8
CHIPS = NX * NY
PLANE = [(dx, dy) for dx in range(NX) for dy in range(NY) if (dx, dy) != (0, 0)]
ROWS = 2560
SLOTS = 24
ROW_BLOCKS = ROWS // BLK
BLOCKS = [4, 4, 6, 6]
FIRST = [sum(BLOCKS[:p]) for p in range(4)]
INNER = 512
TILE = 256
TILES = ROWS // TILE
PARTS = 2
UNIT = 16 * BLK
GROUPS = 99
PHASES = 7


def here():
    a = lax.axis_index("aux")
    return a // 8, (a // 2) % 4, a % 2, lax.axis_index("orb")


def device(x, y, core, z):
    return ((x * 4 + y) * 2 + core, z)


class Copies:
    def __init__(self, send, recv, ruler):
        self.send, self.recv, self.ruler = send, recv, ruler
        self.used, self.phase, self.out, self.due = 0, 0, {}, {}

    def group(self):
        self.used += 1
        return self.used - 1

    def start(self, src, dst, target, group=None, phase=None):
        group = self.group() if group is None else group
        phase = self.phase if phase is None else phase
        copy = pltpu.make_async_remote_copy(
            src_ref=src, dst_ref=dst, send_sem=self.send.at[phase], recv_sem=self.recv.at[group],
            device_id=target, device_id_type=MESH,
        )
        copy.start()
        size = math.prod(src.shape) // UNIT
        self.out[phase] = self.out.get(phase, 0) + size
        self.due[group] = self.due.get(group, 0) + size
        return group

    def take(self, sem, size):
        fits = [(a, r) for a in range(1, NZ + 1) for r in range(1, 9)
                if size % (a * r) == 0 and size // (a * r) <= ROW_BLOCKS]
        a, r = fits[0]
        ref = self.ruler.at[pl.ds(0, a), pl.ds(0, size // (a * r)), pl.ds(0, r * 16)]
        pltpu.make_async_copy(ref, ref, sem).wait()

    def wait(self, groups):
        for group in groups:
            self.take(self.recv.at[group], self.due.pop(group))

    def drain(self):
        for phase, size in self.out.items():
            self.take(self.send.at[phase], size)
        self.out = {}


def peers(x, y, c, z):
    return (
        [device((x + dx) % NX, (y + dy) % NY, c, z) for dx, dy in PLANE]
        + [device(x, y, c, (z + dz) % NZ) for dz in range(1, NZ)]
        + [device(x, y, 1 - c, z)]
    )


def kernel(owner, home, tri, row, col, cnt, out,
           panel, home_v, land0, land1, land2, land3, sel0, sel1, sel2, sel3, cand0, cand1, cand2, cand3, own_t, other_t, lists_v, cnt_v, row_s, col_s, cnt_s, prev, last, run, half,
           other_rows, ip, ip_land, ifull, eown, eoth, eland, ssend, sland, send, recv, local):
    land, sel, cand = (land0, land1, land2, land3), (sel0, sel1, sel2, sel3), (cand0, cand1, cand2, cand3)
    x, y, c, z = here()
    chip = x * 4 + y
    other = device(x, y, 1 - c, z)
    targets = peers(x, y, c, z)
    barrier = pltpu.get_barrier_semaphore()
    for target in targets:
        pl.semaphore_signal(barrier, inc=1, device_id=target, device_id_type=MESH)
    net = Copies(send, recv, panel)
    wait = net.wait

    def piece(p, j):
        n = BLOCKS[p] // 2
        return pl.ds(FIRST[p] + j // 8 * n, n), pl.ds(j % 8 * 16, 16)

    fetch = pltpu.make_async_copy(home, home_v, local.at[0])
    fetch.start()
    here_copies = [
        pltpu.make_async_copy(row, row_s.at[0], local.at[1]),
        pltpu.make_async_copy(col, col_s.at[0], local.at[2]),
        pltpu.make_async_copy(cnt, cnt_s.at[0], local.at[3]),
        pltpu.make_async_copy(tri, own_t, local.at[4]),
    ]
    for copy in here_copies[:3]:
        copy.start()
    fetch.wait()
    for p in range(4):
        land[p][chip] = home_v[piece(p, chip)]
    pl.semaphore_wait(barrier, len(targets))

    scatter = [net.group() for _ in range(4)]

    def deal(p):
        for dx, dy in PLANE:
            tx, ty = (x + dx) % NX, (y + dy) % NY
            net.start(home_v.at[piece(p, tx * 4 + ty)], land[p].at[chip], device(tx, ty, c, z), scatter[p])

    for p in range(4):
        deal(p)
    lists = [
        pltpu.make_async_remote_copy(
            src_ref=src, dst_ref=dst, send_sem=send.at[PHASES + i], recv_sem=recv.at[net.group()],
            device_id=other, device_id_type=MESH,
        )
        for i, (src, dst) in enumerate(((row, lists_v.at[0]), (col, lists_v.at[1]), (cnt, cnt_v)))
    ]
    for copy in lists:
        copy.start()
    here_copies[3].start()

    def look_up(u):
        if u == 0:
            for copy in lists:
                copy.wait()
            to_smem = [
                pltpu.make_async_copy(lists_v.at[0], row_s.at[1], local.at[5]),
                pltpu.make_async_copy(lists_v.at[1], col_s.at[1], local.at[6]),
                pltpu.make_async_copy(cnt_v, cnt_s.at[1], local.at[7]),
            ]
            for copy in to_smem:
                copy.start()
            for copy in here_copies[:3] + to_smem:
                copy.wait()

        @pl.loop(0, SLOTS)
        def _(s):
            mine = row_s[u, 0, 0, s]
            found = jnp.int32(SLOTS)
            for e in range(SLOTS - 1):
                same = jnp.logical_and(row_s[u, 0, 0, e] == mine, e < s)
                found = jnp.where(same, jnp.int32(e), found)
            prev[u, s] = found

        @pl.loop(0, ROW_BLOCKS)
        def _(t):
            found = jnp.int32(SLOTS)
            for e in range(SLOTS):
                same = jnp.logical_and(row_s[u, 0, 0, e] == t, e < cnt_s[u, 0, 0])
                found = jnp.where(same, jnp.int32(e), found)
            last[u, t] = found

        run[u, SLOTS] = jnp.zeros((2 * BLK, BLK), F32)

    def choose(p):
        wait([scatter[p]])
        sel[p][...] = land[p][owner[1 - c] // 2]
        passed = net.start(sel[p], cand[p].at[1], other)
        cand[p][0] = land[p][owner[c] // 2]
        wait([passed])
        panel[(0,) + piece(p, chip)] = cand[p][(owner[c] + c) % 2]

    ring, plane = {}, {}

    def to_plane(p):
        choose(p)
        mine = panel.at[(0,) + piece(p, chip)]
        plane[p] = net.group()
        for dx, dy in PLANE:
            net.start(mine, mine, device((x + dx) % NX, (y + dy) % NY, c, z), plane[p])

    def step(p, k):
        for e in range(2):
            for sign in (1, -1):
                if k > (4 if (sign == 1) == (e == 0) else 3):
                    continue
                if k > 1:
                    wait([ring[p, k - 1, e, sign]])
                n = BLOCKS[p] // 2
                blocks = pl.ds(FIRST[p] + e * n, n)
                ring[p, k, e, sign] = net.start(
                    panel.at[-sign * (k - 1) % NZ, blocks], panel.at[-sign * k % NZ, blocks],
                    device(x, y, c, (z + sign + NZ) % NZ), None, 2)

    column, chunks, first, second, tail = {}, {}, {}, {}, net.group()
    uv = [(x, y), (y, x)]

    def to_column(p):
        choose(p)
        column[p] = net.group()
        for dz in (1, 7, 2, 6, 3, 5, 4):
            net.start(panel.at[(0,) + piece(p, chip)], panel.at[(NZ - dz,) + piece(p, chip)],
                      device(x, y, c, (z + dz) % NZ), column[p])

    def block(p, h, u, v, skip, n):
        u, v = u % 4, v % 4
        return panel.at[(pl.ds(h * 4 + skip, n),) + piece(p, u * 4 + v if h == 0 else v * 4 + u)]

    def push(h, src, u, v, group=None):
        u, v = u % 4, v % 4
        return net.start(src, src, device(u, v, c, z) if h == 0 else device(v, u, c, z), group, 3)

    def begin(p):
        wait([column[p]])
        for h, (u, v) in enumerate(uv):
            src = block(p, h, u, v, 0, 4)
            first[p, h] = [push(h, src, u + 1, v), push(h, src, u + 3, v)]

    def spread(p, q, du):
        for h, (u, v) in enumerate(uv):
            src = block(p, h, u + du, v, 0, 4)
            chunks[p, q, h] = [push(h, src, u, v + 1), push(h, src, u, v + 3)]

    def pass_on(p):
        for h, (u, v) in enumerate(uv):
            up, down = first[p, h]
            second[p, h] = net.group()
            wait([up])
            push(h, block(p, h, u + 3, v, 0, 2), u + 1, v, second[p, h])
            wait([down])
            push(h, block(p, h, u + 1, v, 2, 2), u + 3, v, second[p, h])

    def relay(p, q, du):
        for h, (u, v) in enumerate(uv):
            up, down = chunks[p, q, h]
            wait([up])
            push(h, block(p, h, u + du, v + 3, 0, 2), u, v + 1, tail)
            wait([down])
            push(h, block(p, h, u + du, v + 1, 2, 2), u, v + 3, tail)

    def last_chunk(p):
        wait([second[p, h] for h in range(2)])
        spread(p, 3, 2)

    net.phase = 1
    to_plane(0)
    to_plane(1)
    to_column(2)
    to_column(3)
    wait([plane[0]])
    step(0, 1)
    wait([plane[1]])
    step(1, 1)
    begin(2)
    spread(2, 0, 0)
    tri_copy = net.start(tri, other_t, other, None, 2)
    begin(3)
    spread(3, 0, 0)
    step(0, 2)
    pass_on(2)
    spread(2, 1, 3)
    spread(2, 2, 1)
    relay(2, 0, 0)
    step(1, 2)
    pass_on(3)
    spread(3, 1, 3)
    spread(3, 2, 1)
    relay(3, 0, 0)
    step(0, 3)
    look_up(0)
    last_chunk(2)
    relay(2, 1, 3)
    relay(2, 2, 1)
    step(1, 3)
    last_chunk(3)
    relay(3, 1, 3)
    relay(3, 2, 1)
    relay(2, 3, 2)
    step(0, 4)
    relay(3, 3, 2)
    step(1, 4)
    look_up(1)
    net.phase = 5
    own_rows = [net.start(panel.at[0, pl.ds(0, FIRST[2])], other_rows.at[pl.ds(0, FIRST[2])], other)]
    wait([tail])
    rest = ROW_BLOCKS - FIRST[2]
    own_rows.append(net.start(panel.at[0, pl.ds(FIRST[2], rest)], other_rows.at[pl.ds(FIRST[2], rest)], other))
    for p in range(2):
        wait([ring[p, 3, 0, -1], ring[p, 3, 1, 1], ring[p, 4, 0, 1], ring[p, 4, 1, -1]])

    here_copies[3].wait()
    wait([tri_copy])
    for u, integrals in enumerate((own_t, other_t)):
        @pl.loop(0, SLOTS, step=2)
        def _(s0, u=u, integrals=integrals):
            products = []
            for i in range(2):
                b = col_s[u, 0, 0, s0 + i]
                rows = panel[(b // ROW_BLOCKS + NZ - z) % NZ, b % ROW_BLOCKS]
                t = integrals[:, s0 + i].reshape(2 * BLK, BLK)
                products.append(jnp.dot(t, rows, preferred_element_type=F32))
            for i in range(2):
                run[u, s0 + i] = products[i] + run[u, prev[u, s0 + i]]
    for u in range(2):
        @pl.loop(0, ROW_BLOCKS)
        def _(t, u=u):
            total = run[u, last[u, t]].astype(BF16)
            at = pl.ds(pl.multiple_of(t * BLK, BLK), BLK)
            for p in range(2):
                half[at, pl.ds((2 * u + p) * BLK, BLK)] = total[p * BLK:(p + 1) * BLK]

    for q in range(2):
        if q == 1:
            wait(own_rows)
        rows = (panel[0] if q == 0 else other_rows[...]).reshape(ROWS, BLK)
        part = lax.dot_general(rows, half[...], (((0,), (0,)), ((), ())), preferred_element_type=F32)
        part = part.reshape(CHIPS // 2, 2, 8, INNER)
        for g in range(2):
            ip[g, q * 4:(q + 1) * 4] = part[:, g].reshape(4, 16, INNER).astype(BF16)

    group = [1 - c, c]
    shares, whole = [net.group() for _ in range(2)], [net.group() for _ in range(2)]
    for k in range(2):
        for dz in range(1, NZ):
            to = (z + dz) % NZ
            net.start(ip.at[group[k], to], ip_land.at[k, dz - 1], device(x, y, c, to), shares[k], 4)
    for k in range(2):
        wait([shares[k]])
        total = ip[group[k], z].astype(F32)
        for dz in range(1, NZ):
            total += ip_land[k, dz - 1].astype(F32)
        ifull[k, z] = total.astype(BF16)
        mine = ifull.at[k, z]
        for dz in range(1, NZ):
            net.start(mine, mine, device(x, y, c, (z + dz) % NZ), whole[k], 4)

    per = TILES // PARTS

    def tile(it, t):
        e = lax.dot_general(it, half[t * TILE:(t + 1) * TILE, :], (((1,), (1,)), ((), ())),
                            preferred_element_type=F32)
        e = e.reshape(CHIPS, 8, TILE)
        return jnp.concatenate([e[..., :BLK], e[..., BLK:]], axis=1)

    wait([whole[0]])
    it = ifull[0].reshape(BLK, INNER)
    swaps = []
    for k in range(PARTS):
        for t in range(per):
            eoth[k, :, :, t * BLK:(t + 1) * BLK] = tile(it, k * per + t).astype(BF16)
        swaps.append(net.start(eoth.at[k], eland.at[k], other))
    wait([whole[1]])
    it = ifull[1].reshape(BLK, INNER)
    shares = []
    for k in range(PARTS):
        for t in range(per):
            eown[k, :, :, t * BLK:(t + 1) * BLK] = tile(it, k * per + t)
        wait([swaps[k]])
        for d in range(CHIPS):
            summed = eown[k, d] + eland[k, (d + 8) % CHIPS].astype(F32)
            eown[k, d] = summed
            ssend[k, d] = summed.astype(BF16)
        shares.append(net.group())
        for i, (dx, dy) in enumerate(PLANE):
            tx, ty = (x + dx) % NX, (y + dy) % NY
            net.start(ssend.at[k, (tx * 4 + ty + 8 * c) % CHIPS], sland.at[k, i], device(tx, ty, c, z), shares[k], 6)
    net.drain()
    for k in range(PARTS):
        wait([shares[k]])
        total = eown[k, (chip + 8 * c) % CHIPS]
        for i in range(CHIPS - 1):
            total += sland[k, i].astype(F32)
        for t in range(per):
            at = (k * per + t) * TILE
            out[:, at:at + BLK] = total[0:8, t * BLK:(t + 1) * BLK]
            out[:, at + BLK:at + TILE] = total[8:16, t * BLK:(t + 1) * BLK]


def body(three_index, home_panels, panel_owner, block_row, block_column, block_count):
    anywhere = pl.BlockSpec(memory_space=pl.ANY)
    smem = pl.BlockSpec(memory_space=pltpu.SMEM)
    dma = pltpu.SemaphoreType.DMA
    vm = pltpu.VMEM
    pieces = [(n // 2, 16, BLK) for n in BLOCKS]
    packed = (PARTS, CHIPS, 16, ROWS // 2 // PARTS)
    out = pl.pallas_call(
        kernel,
        name="exchange",
        out_shape=jax.ShapeDtypeStruct((8, ROWS), F32),
        in_specs=[smem] + [anywhere] * 5,
        out_specs=pl.BlockSpec(memory_space=vm),
        scratch_shapes=[
            vm((NZ, ROW_BLOCKS, BLK, BLK), BF16),
            vm((ROW_BLOCKS, BLK, BLK), BF16),
        ] + [
            vm((CHIPS,) + piece, BF16) for piece in pieces
        ] + [
            vm(piece, BF16) for piece in pieces
        ] + [
            vm((2,) + piece, BF16) for piece in pieces
        ] + [
            vm(three_index.shape, BF16),
            vm(three_index.shape, BF16),
            vm((2,) + block_row.shape, jnp.int32),
            vm(block_count.shape, jnp.int32),
            pltpu.SMEM((2,) + block_row.shape, jnp.int32),
            pltpu.SMEM((2,) + block_row.shape, jnp.int32),
            pltpu.SMEM((2,) + block_count.shape, jnp.int32),
            pltpu.SMEM((2, SLOTS), jnp.int32),
            pltpu.SMEM((2, ROW_BLOCKS), jnp.int32),
            vm((2, SLOTS + 1, 2 * BLK, BLK), F32),
            vm((ROWS, INNER), BF16),
            vm((ROW_BLOCKS, BLK, BLK), BF16),
            vm((2, NZ, 16, INNER), BF16),
            vm((2, NZ - 1, 16, INNER), BF16),
            vm((2, NZ, 16, INNER), BF16),
            vm(packed, F32),
            vm(packed, BF16),
            vm(packed, BF16),
            vm(packed, BF16),
            vm((PARTS, CHIPS - 1) + packed[2:], BF16),
            dma((PHASES + 3,)),
            dma((GROUPS,)),
            dma((8,)),
        ],
        compiler_params=pltpu.CompilerParams(collective_id=0, has_side_effects=True, vmem_limit_bytes=60 * 2**20),
    )(panel_owner, home_panels.reshape(ROW_BLOCKS, BLK, BLK), three_index, block_row, block_column, block_count)
    return out.T


def solution(mesh):
    placed = (
        P("aux", "orb", None, None),
        P("aux", "orb", None),
        P(),
        P("aux", "orb", None),
        P("aux", "orb", None),
        P("aux", "orb"),
    )
    return jax.shard_map(
        body, mesh=mesh, in_specs=placed, out_specs=P("orb", "aux"), check_vma=False
    )
```

time: 92.2 us -> 85.2 us (0.924)
  Pallas kernels: 89.8 us -> 82.8 us
    pallas_call x1, Pallas kernels: 89.8 us -> 82.8 us  [body(): pl.pallas_call(kernel, name='exchange', out_shape=jax.ShapeDtypeStruct((8...]
where the time goes in v3:
time: 85.2 us; the launch traced here: 85 us
  Pallas kernels  82.8 us (97%)
  local copies, waits for them, and re-layouts  1.53 us (2%)
    pallas_call x1, Pallas kernels, body(): pl.pallas_call(kernel, name='exchange', out_shape=jax.ShapeDtypeStruct((8...  82.8 us

profile of v3, /device:TPU:1, one launch (start us, length us, event | category | flops | bytes accessed | tf_op | source)
XLA Modules:
  0.0 85.0 jit_solution(5153721513323581892)
XLA Ops:
  0.7 82.8 %exchange.1 = f32[8,2560]{1,0:T(8,128)} custom-call(s32[32]{0:T(128)} %owner.1, bf16[20,128,128]{2,1,0:T(8,128)(2,1)} %bitcast.2, bf16[2,24,128,128]{3,2,1,0:T(8,128)(2,1)} %tri.1, s32[1,1,24]{2,1,0:T(1,128)} %row.1, s32[1,1,24]{2,1,0:T(1,128)} %col.1, s32[1,1]{1,0:T(1,128)S(6)} %copy.8.cnt), custom_call_target="tpu_custom_call" | custom-call | tf_op jit(solution)/shard_map/exchange/pallas_call | solution.py:394
  83.5 1.5 %copy.9 = f32[2560,8]{0,1:T(8,128)} copy(f32[2560,8]{0,1:T(8,128)} %bitcast.3) | data formatting | bytes 163840

commit v4 on v3

--- a/solution.py
+++ b/solution.py
@@ -46,7 +46,7 @@
         self.used += 1
         return self.used - 1
 
-    def start(self, src, dst, target, group=None, phase=None):
+    def start(self, src, dst, target, group=None, phase=None, counted=True):
         group = self.group() if group is None else group
         phase = self.phase if phase is None else phase
         copy = pltpu.make_async_remote_copy(
@@ -54,7 +54,7 @@
             device_id=target, device_id_type=MESH,
         )
         copy.start()
-        size = math.prod(src.shape) // UNIT
+        size = math.prod(src.shape) // UNIT if counted else 0
         self.out[phase] = self.out.get(phase, 0) + size
         self.due[group] = self.due.get(group, 0) + size
         return group
@@ -84,8 +84,8 @@
     )
 
 
-def kernel(owner, home, tri, row, col, cnt, out,
-           panel, home_v, land0, land1, land2, land3, sel0, sel1, sel2, sel3, cand0, cand1, cand2, cand3, own_t, other_t, lists_v, cnt_v, row_s, col_s, cnt_s, prev, last, run, half,
+def kernel(owner_h, home, tri, row, col, cnt, out,
+           panel, owner, home_v, land0, land1, land2, land3, sel0, sel1, sel2, sel3, cand0, cand1, cand2, cand3, own_t, other_t, lists_v, cnt_v, row_s, col_s, cnt_s, prev, last, run, half,
            other_rows, ip, ip_land, ifull, eown, eoth, eland, ssend, sland, send, recv, local):
     land, sel, cand = (land0, land1, land2, land3), (sel0, sel1, sel2, sel3), (cand0, cand1, cand2, cand3)
     x, y, c, z = here()
@@ -110,11 +110,51 @@
         pltpu.make_async_copy(cnt, cnt_s.at[0], local.at[3]),
         pltpu.make_async_copy(tri, own_t, local.at[4]),
     ]
+    own_list = pltpu.make_async_copy(owner_h, owner, local.at[8])
+    own_list.start()
     for copy in here_copies[:3]:
         copy.start()
+    own_list.wait()
+    def look_up(u):
+        if u == 0:
+            for copy in here_copies[:3]:
+                copy.wait()
+        else:
+            for copy in lists:
+                copy.wait()
+            to_smem = [
+                pltpu.make_async_copy(lists_v.at[0], row_s.at[1], local.at[5]),
+                pltpu.make_async_copy(lists_v.at[1], col_s.at[1], local.at[6]),
+                pltpu.make_async_copy(cnt_v, cnt_s.at[1], local.at[7]),
+            ]
+            for copy in to_smem:
+                copy.start()
+            for copy in to_smem:
+                copy.wait()
+
+        @pl.loop(0, SLOTS)
+        def _(s):
+            mine = row_s[u, 0, 0, s]
+            found = jnp.int32(SLOTS)
+            for e in range(SLOTS - 1):
+                same = jnp.logical_and(row_s[u, 0, 0, e] == mine, e < s)
+                found = jnp.where(same, jnp.int32(e), found)
+            prev[u, s] = found
+
+        @pl.loop(0, ROW_BLOCKS)
+        def _(t):
+            found = jnp.int32(SLOTS)
+            for e in range(SLOTS):
+                same = jnp.logical_and(row_s[u, 0, 0, e] == t, e < cnt_s[u, 0, 0])
+                found = jnp.where(same, jnp.int32(e), found)
+            last[u, t] = found
+
+        run[u, SLOTS] = jnp.zeros((2 * BLK, BLK), F32)
+
     fetch.wait()
     for p in range(4):
         land[p][chip] = home_v[piece(p, chip)]
+    look_up(0)
     pl.semaphore_wait(barrier, len(targets))
 
     scatter = [net.group() for _ in range(4)]
@@ -137,38 +177,7 @@
         copy.start()
     here_copies[3].start()
 
-    def look_up(u):
-        if u == 0:
-            for copy in lists:
-                copy.wait()
-            to_smem = [
-                pltpu.make_async_copy(lists_v.at[0], row_s.at[1], local.at[5]),
-                pltpu.make_async_copy(lists_v.at[1], col_s.at[1], local.at[6]),
-                pltpu.make_async_copy(cnt_v, cnt_s.at[1], local.at[7]),
-            ]
-            for copy in to_smem:
-                copy.start()
-            for copy in here_copies[:3] + to_smem:
-                copy.wait()
-
-        @pl.loop(0, SLOTS)
-        def _(s):
-            mine = row_s[u, 0, 0, s]
-            found = jnp.int32(SLOTS)
-            for e in range(SLOTS - 1):
-                same = jnp.logical_and(row_s[u, 0, 0, e] == mine, e < s)
-                found = jnp.where(same, jnp.int32(e), found)
-            prev[u, s] = found
-
-        @pl.loop(0, ROW_BLOCKS)
-        def _(t):
-            found = jnp.int32(SLOTS)
-            for e in range(SLOTS):
-                same = jnp.logical_and(row_s[u, 0, 0, e] == t, e < cnt_s[u, 0, 0])
-                found = jnp.where(same, jnp.int32(e), found)
-            last[u, t] = found
-
-        run[u, SLOTS] = jnp.zeros((2 * BLK, BLK), F32)
+    look_up(1)
 
     def choose(p):
         wait([scatter[p]])
@@ -275,7 +284,6 @@
     spread(3, 2, 1)
     relay(3, 0, 0)
     step(0, 3)
-    look_up(0)
     last_chunk(2)
     relay(2, 1, 3)
     relay(2, 2, 1)
@@ -287,7 +295,6 @@
     step(0, 4)
     relay(3, 3, 2)
     step(1, 4)
-    look_up(1)
     net.phase = 5
     own_rows = [net.start(panel.at[0, pl.ds(0, FIRST[2])], other_rows.at[pl.ds(0, FIRST[2])], other)]
     wait([tail])
@@ -299,23 +306,24 @@
     here_copies[3].wait()
     wait([tri_copy])
     for u, integrals in enumerate((own_t, other_t)):
-        @pl.loop(0, SLOTS, step=2)
+        @pl.loop(0, SLOTS, step=8)
         def _(s0, u=u, integrals=integrals):
             products = []
-            for i in range(2):
+            for i in range(8):
                 b = col_s[u, 0, 0, s0 + i]
                 rows = panel[(b // ROW_BLOCKS + NZ - z) % NZ, b % ROW_BLOCKS]
                 t = integrals[:, s0 + i].reshape(2 * BLK, BLK)
                 products.append(jnp.dot(t, rows, preferred_element_type=F32))
-            for i in range(2):
+            for i in range(8):
                 run[u, s0 + i] = products[i] + run[u, prev[u, s0 + i]]
     for u in range(2):
-        @pl.loop(0, ROW_BLOCKS)
+        @pl.loop(0, ROW_BLOCKS, step=4)
         def _(t, u=u):
-            total = run[u, last[u, t]].astype(BF16)
-            at = pl.ds(pl.multiple_of(t * BLK, BLK), BLK)
-            for p in range(2):
-                half[at, pl.ds((2 * u + p) * BLK, BLK)] = total[p * BLK:(p + 1) * BLK]
+            for i in range(4):
+                total = run[u, last[u, t + i]].astype(BF16)
+                at = pl.ds(pl.multiple_of((t + i) * BLK, BLK), BLK)
+                for p in range(2):
+                    half[at, pl.ds((2 * u + p) * BLK, BLK)] = total[p * BLK:(p + 1) * BLK]
 
     for q in range(2):
         if q == 1:
@@ -326,15 +334,14 @@
         for g in range(2):
             ip[g, q * 4:(q + 1) * 4] = part[:, g].reshape(4, 16, INNER).astype(BF16)
 
-    group = [1 - c, c]
     shares, whole = [net.group() for _ in range(2)], [net.group() for _ in range(2)]
     for k in range(2):
         for dz in range(1, NZ):
             to = (z + dz) % NZ
-            net.start(ip.at[group[k], to], ip_land.at[k, dz - 1], device(x, y, c, to), shares[k], 4)
+            net.start(ip.at[k, to], ip_land.at[k, dz - 1], device(x, y, c, to), shares[k], 4)
     for k in range(2):
         wait([shares[k]])
-        total = ip[group[k], z].astype(F32)
+        total = ip[k, z].astype(F32)
         for dz in range(1, NZ):
             total += ip_land[k, dz - 1].astype(F32)
         ifull[k, z] = total.astype(BF16)
@@ -350,28 +357,34 @@
         e = e.reshape(CHIPS, 8, TILE)
         return jnp.concatenate([e[..., :BLK], e[..., BLK:]], axis=1)
 
-    wait([whole[0]])
-    it = ifull[0].reshape(BLK, INNER)
-    swaps = []
-    for k in range(PARTS):
-        for t in range(per):
-            eoth[k, :, :, t * BLK:(t + 1) * BLK] = tile(it, k * per + t).astype(BF16)
-        swaps.append(net.start(eoth.at[k], eland.at[k], other))
-    wait([whole[1]])
-    it = ifull[1].reshape(BLK, INNER)
-    shares = []
-    for k in range(PARTS):
-        for t in range(per):
-            eown[k, :, :, t * BLK:(t + 1) * BLK] = tile(it, k * per + t)
-        wait([swaps[k]])
-        for d in range(CHIPS):
-            summed = eown[k, d] + eland[k, (d + 8) % CHIPS].astype(F32)
-            eown[k, d] = summed
-            ssend[k, d] = summed.astype(BF16)
-        shares.append(net.group())
-        for i, (dx, dy) in enumerate(PLANE):
-            tx, ty = (x + dx) % NX, (y + dy) % NY
-            net.start(ssend.at[k, (tx * 4 + ty + 8 * c) % CHIPS], sland.at[k, i], device(tx, ty, c, z), shares[k], 6)
+    swaps = [net.group() for _ in range(PARTS)]
+    shares = [net.group() for _ in range(PARTS)]
+    for k in range(2):
+        wait([whole[k]])
+        it = ifull[k].reshape(BLK, INNER)
+
+        @pl.when(c != k)
+        def _(k=k, it=it):
+            for part in range(PARTS):
+                for t in range(per):
+                    eoth[part, :, :, t * BLK:(t + 1) * BLK] = tile(it, part * per + t).astype(BF16)
+                net.start(eoth.at[part], eland.at[part], other, swaps[part], counted=k == 0)
+
+        @pl.when(c == k)
+        def _(k=k, it=it):
+            for part in range(PARTS):
+                for t in range(per):
+                    eown[part, :, :, t * BLK:(t + 1) * BLK] = tile(it, part * per + t)
+            for part in range(PARTS):
+                net.take(recv.at[swaps[part]], math.prod(eoth.shape[1:]) // UNIT)
+                for d in range(CHIPS):
+                    summed = eown[part, d] + eland[part, (d + 8) % CHIPS].astype(F32)
+                    eown[part, d] = summed
+                    ssend[part, d] = summed.astype(BF16)
+                for i, (dx, dy) in enumerate(PLANE):
+                    tx, ty = (x + dx) % NX, (y + dy) % NY
+                    net.start(ssend.at[part, (tx * 4 + ty + 8 * c) % CHIPS], sland.at[part, i],
+                              device(tx, ty, c, z), shares[part], 6, k == 0)
     net.drain()
     for k in range(PARTS):
         wait([shares[k]])
@@ -395,10 +408,11 @@
         kernel,
         name="exchange",
         out_shape=jax.ShapeDtypeStruct((8, ROWS), F32),
-        in_specs=[smem] + [anywhere] * 5,
+        in_specs=[anywhere] * 6,
         out_specs=pl.BlockSpec(memory_space=vm),
         scratch_shapes=[
             vm((NZ, ROW_BLOCKS, BLK, BLK), BF16),
+            pltpu.SMEM((32,), jnp.int32),
             vm((ROW_BLOCKS, BLK, BLK), BF16),
         ] + [
             vm((CHIPS,) + piece, BF16) for piece in pieces
@@ -429,10 +443,13 @@
             vm((PARTS, CHIPS - 1) + packed[2:], BF16),
             dma((PHASES + 3,)),
             dma((GROUPS,)),
-            dma((8,)),
+            dma((9,)),
         ],
-        compiler_params=pltpu.CompilerParams(collective_id=0, has_side_effects=True, vmem_limit_bytes=60 * 2**20),
-    )(panel_owner, home_panels.reshape(ROW_BLOCKS, BLK, BLK), three_index, block_row, block_column, block_count)
+        compiler_params=pltpu.CompilerParams(collective_id=0, has_side_effects=True, vmem_limit_bytes=48 * 2**20),
+    )(*[
+        pltpu.with_memory_space_constraint(value, pltpu.HBM)
+        for value in (panel_owner, home_panels.reshape(ROW_BLOCKS, BLK, BLK), three_index, block_row, block_column)
+    ], block_count)
     return out.T
 
 

time: 85.2 us -> 79.2 us (0.930)
  Pallas kernels: 82.8 us -> 77.8 us
  local copies, waits for them, and re-layouts: 1.53 us -> 0.64 us
    pallas_call x1, Pallas kernels: 82.8 us -> 77.8 us  [body(): pl.pallas_call(kernel, name='exchange', out_shape=jax.ShapeDtypeStruct((8...]
    unnamed x1, local copies, waits for them, and re-layouts: 1.53 us -> 0.64 us
where the time goes in v4:
time: 79.2 us; the launch traced here: 79.1 us
  Pallas kernels  77.8 us (98%)
    pallas_call x1, Pallas kernels, body(): pl.pallas_call(kernel, name='exchange', out_shape=jax.ShapeDtypeStruct((8...  77.8 us

profile of v4, /device:TPU:1, one launch (start us, length us, event | category | flops | bytes accessed | tf_op | source)
XLA Modules:
  0.0 79.1 jit_solution(4244654973585335427)
XLA Ops:
  0.7 77.8 %exchange.1 = f32[8,2560]{1,0:T(8,128)S(1)} custom-call(s32[32]{0:T(128)} %owner_h.1, bf16[20,128,128]{2,1,0:T(8,128)(2,1)} %bitcast.3, bf16[2,24,128,128]{3,2,1,0:T(8,128)(2,1)} %tri.1, s32[1,1,24]{2,1,0:T(1,128)} %row.1, s32[1,1,24]{2,1,0:T(1,128)} %col.1, s32[1,1]{1,0:T(1,128)S(6)} %copy.8.cnt), custom_call_target="tpu_custom_call" | custom-call | tf_op jit(solution)/shard_map/exchange/pallas_call | solution.py:407
  78.5 0.6 copy.9

commit v5 on v4

--- a/solution.py
+++ b/solution.py
@@ -13,7 +13,8 @@
 BLK = 128
 NX, NY, NZ = 4, 4, 8
 CHIPS = NX * NY
-PLANE = [(dx, dy) for dx in range(NX) for dy in range(NY) if (dx, dy) != (0, 0)]
+PLANE = [(2, 2), (2, 1), (2, 3), (1, 2), (3, 2), (2, 0), (0, 2), (1, 1), (1, 3), (3, 1), (3, 3), (1, 0), (3, 0), (0, 1), (0, 3)]
+LINE = (4, 3, 5, 2, 6, 1, 7)
 ROWS = 2560
 SLOTS = 24
 ROW_BLOCKS = ROWS // BLK
@@ -79,7 +80,7 @@
 def peers(x, y, c, z):
     return (
         [device((x + dx) % NX, (y + dy) % NY, c, z) for dx, dy in PLANE]
-        + [device(x, y, c, (z + dz) % NZ) for dz in range(1, NZ)]
+        + [device(x, y, c, (z + dz) % NZ) for dz in LINE]
         + [device(x, y, 1 - c, z)]
     )
 
@@ -215,7 +216,7 @@
     def to_column(p):
         choose(p)
         column[p] = net.group()
-        for dz in (1, 7, 2, 6, 3, 5, 4):
+        for dz in LINE:
             net.start(panel.at[(0,) + piece(p, chip)], panel.at[(NZ - dz,) + piece(p, chip)],
                       device(x, y, c, (z + dz) % NZ), column[p])
 
@@ -336,7 +337,7 @@
 
     shares, whole = [net.group() for _ in range(2)], [net.group() for _ in range(2)]
     for k in range(2):
-        for dz in range(1, NZ):
+        for dz in LINE:
             to = (z + dz) % NZ
             net.start(ip.at[k, to], ip_land.at[k, dz - 1], device(x, y, c, to), shares[k], 4)
     for k in range(2):
@@ -346,7 +347,7 @@
             total += ip_land[k, dz - 1].astype(F32)
         ifull[k, z] = total.astype(BF16)
         mine = ifull.at[k, z]
-        for dz in range(1, NZ):
+        for dz in LINE:
             net.start(mine, mine, device(x, y, c, (z + dz) % NZ), whole[k], 4)
 
     per = TILES // PARTS

time: 79.2 us -> 76.5 us (0.966)
  Pallas kernels: 77.8 us -> 75.1 us
    pallas_call x1, Pallas kernels: 77.8 us -> 75.1 us  [body(): pl.pallas_call(kernel, name='exchange', out_shape=jax.ShapeDtypeStruct((8...]
where the time goes in v5:
time: 76.5 us; the launch traced here: 76.4 us
  Pallas kernels  75.1 us (98%)
    pallas_call x1, Pallas kernels, body(): pl.pallas_call(kernel, name='exchange', out_shape=jax.ShapeDtypeStruct((8...  75.1 us

profile of v5, /device:TPU:1, one launch (start us, length us, event | category | flops | bytes accessed | tf_op | source)
XLA Modules:
  0.0 76.4 jit_solution(6624274163329845997)
XLA Ops:
  0.7 75.1 %exchange.1 = f32[8,2560]{1,0:T(8,128)S(1)} custom-call(s32[32]{0:T(128)} %owner_h.1, bf16[20,128,128]{2,1,0:T(8,128)(2,1)} %bitcast.3, bf16[2,24,128,128]{3,2,1,0:T(8,128)(2,1)} %tri.1, s32[1,1,24]{2,1,0:T(1,128)} %row.1, s32[1,1,24]{2,1,0:T(1,128)} %col.1, s32[1,1]{1,0:T(1,128)S(6)} %copy.8.cnt), custom_call_target="tpu_custom_call" | custom-call | tf_op jit(solution)/shard_map/exchange/pallas_call | solution.py:408
  75.7 0.6 copy.9

commit v6 on v5

--- a/solution.py
+++ b/solution.py
@@ -165,7 +165,7 @@
             tx, ty = (x + dx) % NX, (y + dy) % NY
             net.start(home_v.at[piece(p, tx * 4 + ty)], land[p].at[chip], device(tx, ty, c, z), scatter[p])
 
-    for p in range(4):
+    for p in (2, 0, 3, 1):
         deal(p)
     lists = [
         pltpu.make_async_remote_copy(
@@ -261,36 +261,36 @@
         spread(p, 3, 2)
 
     net.phase = 1
+    to_column(2)
     to_plane(0)
+    to_column(3)
     to_plane(1)
-    to_column(2)
-    to_column(3)
+    begin(2)
+    spread(2, 0, 0)
     wait([plane[0]])
     step(0, 1)
+    begin(3)
+    spread(3, 0, 0)
+    tri_copy = net.start(tri, other_t, other, None, 2)
     wait([plane[1]])
     step(1, 1)
-    begin(2)
-    spread(2, 0, 0)
-    tri_copy = net.start(tri, other_t, other, None, 2)
-    begin(3)
-    spread(3, 0, 0)
-    step(0, 2)
     pass_on(2)
     spread(2, 1, 3)
     spread(2, 2, 1)
     relay(2, 0, 0)
-    step(1, 2)
+    step(0, 2)
     pass_on(3)
     spread(3, 1, 3)
     spread(3, 2, 1)
     relay(3, 0, 0)
-    step(0, 3)
+    step(1, 2)
     last_chunk(2)
     relay(2, 1, 3)
     relay(2, 2, 1)
-    step(1, 3)
+    step(0, 3)
     last_chunk(3)
     relay(3, 1, 3)
+    step(1, 3)
     relay(3, 2, 1)
     relay(2, 3, 2)
     step(0, 4)

time: 76.5 us -> 75.4 us (0.986)
  Pallas kernels: 75.1 us -> 74 us
    pallas_call x1, Pallas kernels: 75.1 us -> 74 us  [body(): pl.pallas_call(kernel, name='exchange', out_shape=jax.ShapeDtypeStruct((8...]
where the time goes in v6:
time: 75.4 us; the launch traced here: 75.3 us
  Pallas kernels  74 us (98%)
    pallas_call x1, Pallas kernels, body(): pl.pallas_call(kernel, name='exchange', out_shape=jax.ShapeDtypeStruct((8...  74 us

profile of v6, /device:TPU:1, one launch (start us, length us, event | category | flops | bytes accessed | tf_op | source)
XLA Modules:
  0.0 75.3 jit_solution(2302487204794183137)
XLA Ops:
  0.7 74.0 %exchange.1 = f32[8,2560]{1,0:T(8,128)S(1)} custom-call(s32[32]{0:T(128)} %owner_h.1, bf16[20,128,128]{2,1,0:T(8,128)(2,1)} %bitcast.3, bf16[2,24,128,128]{3,2,1,0:T(8,128)(2,1)} %tri.1, s32[1,1,24]{2,1,0:T(1,128)} %row.1, s32[1,1,24]{2,1,0:T(1,128)} %col.1, s32[1,1]{1,0:T(1,128)S(6)} %copy.8.cnt), custom_call_target="tpu_custom_call" | custom-call | tf_op jit(solution)/shard_map/exchange/pallas_call | solution.py:408
  74.7 0.6 copy.9

commit v7 on v6

--- a/solution.py
+++ b/solution.py
@@ -178,6 +178,7 @@
         copy.start()
     here_copies[3].start()
 
+    tri_copy = net.start(tri, other_t, other, None, 2)
     look_up(1)
 
     def choose(p):
@@ -271,23 +272,22 @@
     step(0, 1)
     begin(3)
     spread(3, 0, 0)
-    tri_copy = net.start(tri, other_t, other, None, 2)
     wait([plane[1]])
     step(1, 1)
     pass_on(2)
     spread(2, 1, 3)
     spread(2, 2, 1)
+    step(0, 2)
     relay(2, 0, 0)
-    step(0, 2)
     pass_on(3)
     spread(3, 1, 3)
     spread(3, 2, 1)
+    step(1, 2)
     relay(3, 0, 0)
-    step(1, 2)
     last_chunk(2)
     relay(2, 1, 3)
+    step(0, 3)
     relay(2, 2, 1)
-    step(0, 3)
     last_chunk(3)
     relay(3, 1, 3)
     step(1, 3)

time: 75.4 us -> 75.4 us (level)
  no operation moved by 1% of the time
where the time goes in v7:
time: 75.4 us; the launch traced here: 75.3 us
  Pallas kernels  74 us (98%)
    pallas_call x1, Pallas kernels, body(): pl.pallas_call(kernel, name='exchange', out_shape=jax.ShapeDtypeStruct((8...  74 us

profile of v7, /device:TPU:1, one launch (start us, length us, event | category | flops | bytes accessed | tf_op | source)
XLA Modules:
  0.0 75.3 jit_solution(7745689035126134806)
XLA Ops:
  0.7 74.0 %exchange.1 = f32[8,2560]{1,0:T(8,128)S(1)} custom-call(s32[32]{0:T(128)} %owner_h.1, bf16[20,128,128]{2,1,0:T(8,128)(2,1)} %bitcast.3, bf16[2,24,128,128]{3,2,1,0:T(8,128)(2,1)} %tri.1, s32[1,1,24]{2,1,0:T(1,128)} %row.1, s32[1,1,24]{2,1,0:T(1,128)} %col.1, s32[1,1]{1,0:T(1,128)S(6)} %copy.8.cnt), custom_call_target="tpu_custom_call" | custom-call | tf_op jit(solution)/shard_map/exchange/pallas_call | solution.py:408
  74.7 0.6 copy.9
